TPU v7x, 128 devices: a whole 4x4x4 slice. The times are simulated.
128 devices in a mesh: expert: 8 (over z_lo, y), dp: 16 (over z_hi, x, core).
Axes of the slice: x: 4, y: 4, z: 4 (z_hi: 2, z_lo: 2; z = z_hi * 2 + z_lo), core: 2. Of those that a mesh axis runs over, the one named last changes fastest.
Arguments:
- tokens: bfloat16 [2048, 7168], P('dp', 'expert'), may hold values from -6 to 6
- grad_out: bfloat16 [2048, 7168], P('dp', 'expert'), may hold values from -6 to 6
- expert_ids: int32 [2048, 2], P('dp'), may hold values from -1 to 7, as said below
- route_weights: float32 [2048, 2], P('dp'), may hold values from 0.1 to 1
- w_gate: bfloat16 [8, 7168, 2048], P('expert', 'dp'), may hold values from -0.0625 to 0.0625
- w_up: bfloat16 [8, 7168, 2048], P('expert', 'dp'), may hold values from -0.0625 to 0.0625
- w_down: bfloat16 [8, 2048, 7168], P('expert', None, 'dp'), may hold values from -0.125 to 0.125
Outputs:
- grad_tokens: bfloat16 [2048, 7168], P('dp', 'expert')
- grad_gate: bfloat16 [8, 7168, 2048], P('expert', 'dp')
- grad_up: bfloat16 [8, 7168, 2048], P('expert', 'dp')
- grad_down: bfloat16 [8, 2048, 7168], P('expert', None, 'dp')
Inputs may be any that keep to these rules, and one draw needn't show every extreme that they name: expert_ids[t, 0] is an expert; expert_ids[t, 1] is another expert or -1. Within each block of 128 rows (the tokens of one index of dp) no expert appears in more than 64 rows, and one expert, the same in every block, appears in exactly 64 rows, each of which has -1 as its second entry.
All inputs are finite; a program needn't handle non-finite values.
Results may differ from a plain program's by a relative error of at most 0.03.
Values may be sent and summed in bfloat16 or wider, within the bound.
A program may use at most 128 MiB of HBM per device.

v0:
```python
import math
import jax
import jax.numpy as jnp
from jax import lax
from jax.sharding import PartitionSpec as P


def body(tokens, grad_out, expert_ids, route_weights, w_gate, w_up, w_down):
    experts = lax.axis_size("expert")
    groups = lax.axis_size("dp")
    tok_rows = tokens.shape[0]
    capacity = tok_rows // 2
    hidden = w_gate.shape[2]
    slots = groups * capacity
    expert_index = lax.axis_index("expert")
    inv_root = 1.0 / math.sqrt(tok_rows * groups)
    rows_first = (((0,), (0,)), ((), ()))
    last_dims = (((1,), (1,)), ((), ()))
    routed = expert_ids >= 0
    matches = (
        expert_ids[:, :, None] == jnp.arange(experts, dtype=jnp.int32)[None, None, :]
    ).astype(jnp.int32)
    flat_match = matches.reshape(tok_rows * 2, experts)
    position = jnp.sum(flat_match * (jnp.cumsum(flat_match, axis=0) - 1), axis=1).reshape(
        tok_rows, 2
    )
    slot_ids = jnp.where(routed, expert_ids * capacity + position, -1)
    slot_match = (
        slot_ids[None, :, :] == jnp.arange(experts * capacity, dtype=jnp.int32)[:, None, None]
    ).astype(jnp.float32)
    dispatch = jnp.sum(slot_match, axis=2).astype(jnp.bfloat16)
    slot_weight = jnp.einsum("stk,tk->s", slot_match, route_weights)
    own_weight = lax.dynamic_slice_in_dim(slot_weight, expert_index * capacity, capacity)
    send_x = (
        jnp.dot(dispatch, tokens, preferred_element_type=jnp.float32)
        .astype(jnp.bfloat16)
        .reshape(experts, capacity, -1)
    )
    send_g = (
        jnp.dot(dispatch, grad_out, preferred_element_type=jnp.float32)
        .astype(jnp.bfloat16)
        .reshape(experts, capacity, -1)
    )
    recv_x, recv_g = (
        lax.all_to_all(
            lax.all_to_all(send_x, "expert", split_axis=0, concat_axis=2, tiled=True),
            "dp",
            split_axis=2,
            concat_axis=1,
            tiled=True,
        ),
        lax.all_to_all(
            lax.all_to_all(send_g, "expert", split_axis=0, concat_axis=2, tiled=True),
            "dp",
            split_axis=2,
            concat_axis=1,
            tiled=True,
        ),
    )
    feature_rows = recv_x.reshape(slots, -1)
    grad_rows = recv_g.reshape(slots, -1)
    gate_shard = w_gate[0]
    up_shard = w_up[0]
    down_shard = w_down[0]
    shard_width = gate_shard.shape[0]
    x_block = feature_rows
    g_block = grad_rows
    gate = jnp.dot(x_block, gate_shard, preferred_element_type=jnp.float32)
    upper = jnp.dot(x_block, up_shard, preferred_element_type=jnp.float32)
    back = lax.dot_general(g_block, down_shard, last_dims, preferred_element_type=jnp.float32)
    mine = lax.psum_scatter(
        jnp.concatenate([gate, upper, back], axis=1).astype(jnp.bfloat16),
        "dp",
        scatter_dimension=0,
        tiled=True,
    ).astype(jnp.float32)
    gate = mine[:, :hidden]
    upper = mine[:, hidden : 2 * hidden]
    back = mine[:, 2 * hidden :] * own_weight[:, None]
    sigmoid_gate = jax.nn.sigmoid(gate)
    scaled = own_weight[:, None] * gate * sigmoid_gate * upper
    d_gate = back * upper * sigmoid_gate * (1.0 + gate * (1.0 - sigmoid_gate))
    d_up = back * gate * sigmoid_gate
    local = jnp.concatenate([scaled, d_gate, d_up], axis=1).astype(jnp.bfloat16)
    piece = lax.all_gather(local, "dp", axis=0, tiled=True)
    x_block = feature_rows
    g_block = grad_rows
    scaled = piece[:, :hidden]
    d_gate = piece[:, hidden : 2 * hidden]
    d_up = piece[:, 2 * hidden :]
    grad_g = lax.dot_general(x_block, d_gate, rows_first, preferred_element_type=jnp.float32)
    grad_u = lax.dot_general(x_block, d_up, rows_first, preferred_element_type=jnp.float32)
    grad_d = lax.dot_general(scaled, g_block, rows_first, preferred_element_type=jnp.float32)
    block_dx = lax.dot_general(
        d_gate, gate_shard, last_dims, preferred_element_type=jnp.float32
    ) + lax.dot_general(d_up, up_shard, last_dims, preferred_element_type=jnp.float32)
    dx_rows = block_dx.astype(jnp.bfloat16)
    grad_g, grad_u, grad_d, dx_rows = (grad_g, grad_u, grad_d, dx_rows)
    returned = lax.all_to_all(
        lax.all_to_all(
            dx_rows.reshape(1, slots, shard_width), "dp", split_axis=1, concat_axis=2, tiled=True
        ),
        "expert",
        split_axis=2,
        concat_axis=0,
        tiled=True,
    )
    returned = returned.reshape(experts * capacity, -1)
    grad_tokens = lax.dot_general(
        dispatch, returned, rows_first, preferred_element_type=jnp.float32
    ).astype(jnp.bfloat16)
    grad_gate = (grad_g * inv_root).astype(jnp.bfloat16)[None]
    grad_up = (grad_u * inv_root).astype(jnp.bfloat16)[None]
    grad_down = (grad_d * inv_root).astype(jnp.bfloat16)[None]
    return (grad_tokens, grad_gate, grad_up, grad_down)


def solution(mesh):
    in_specs = (
        P("dp", "expert"),
        P("dp", "expert"),
        P("dp", None),
        P("dp", None),
        P("expert", "dp", None),
        P("expert", "dp", None),
        P("expert", None, "dp"),
    )
    out_specs = (
        P("dp", "expert"),
        P("expert", "dp", None),
        P("expert", "dp", None),
        P("expert", None, "dp"),
    )
    return jax.shard_map(body, mesh=mesh, in_specs=in_specs, out_specs=out_specs, check_vma=False)
```

profile of v0, /device:TPU:1, one launch (start us, length us, event | category | flops | bytes accessed | tf_op | source)
XLA Modules:
  0.0 595.4 jit_solution(15682744833489243268)
XLA Ops:
  10.3 2.3 convolution_convert_fusion.3
  12.6 6.4 %all-to-all-start.2 = ((bf16[8,64,896]{2,1,0:T(8,128)(2,1)}), bf16[8,64,896]{2,1,0:T(8,128)(2,1)S(1)}, u32[]{:S(2)}, u32[]{:S(2)}) async-start(bf16[8,64,896]{2,1,0:T(8,128)(2,1)} %bitcast.12), calls=%async_computation.2 | async-start | bytes 1835008 | tf_op jit(solution)/shard_map/all_to_all | solution.py:53
  19.0 1.3 convolution_convert_fusion.4
  20.3 13.1 %all-to-all-done.2 = bf16[8,64,896]{2,1,0:T(8,128)(2,1)S(1)} async-done(((bf16[8,64,896]{2,1,0:T(8,128)(2,1)}), bf16[8,64,896]{2,1,0:T(8,128)(2,1)S(1)}, u32[]{:S(2)}, u32[]{:S(2)}) %all-to-all-start.2) | async-done | bytes 917536 | tf_op jit(solution)/shard_map/all_to_all | solution.py:53
  34.3 3.6 all-to-all-start
  37.9 2.6 copy.97
  40.4 11.1 %reshape.65 = bf16[1,64,7168]{1,0,2:T(2,128)(2,1)} reshape(bf16[1,64,8,896]{1,3,2,0:T(8,128)(2,1)} %copy.97) | data formatting | bytes 1835008 | tf_op jit(solution)/shard_map/all_to_all | solution.py:53
  52.1 41.0 %reduce.2 = bf16[7168,64]{1,0:T(8,128)(2,1)} reduce(bf16[7168,1,64]{2,1,0:T(2,128)(2,1)} %bitcast.92, bf16[]{:T(256)} %broadcast.46), dimensions={1}, to_apply=%bitcast.70.reduce_sub_computation | reduce | bytes 1835010
  93.1 4.3 reshape.68
  97.3 8.5 %all-to-all-start.3 = ((bf16[16,2,14336]{2,1,0:T(2,128)(2,1)}), bf16[16,2,14336]{2,1,0:T(2,128)(2,1)}, u32[]{:S(2)}, u32[]{:S(2)}) async-start(bf16[16,2,14336]{2,1,0:T(2,128)(2,1)} %reshape.68), calls=%async_computation.3 | async-start | bytes 1835008 | tf_op jit(solution)/shard_map/all_to_all | solution.py:52
  105.9 1.7 copy.96
  107.5 11.1 %reshape.64 = bf16[1,64,7168]{1,0,2:T(2,128)(2,1)} reshape(bf16[1,64,8,896]{1,3,2,0:T(8,128)(2,1)} %copy.96) | data formatting | bytes 1835008 | tf_op jit(solution)/shard_map/all_to_all | solution.py:46
  118.7 41.0 %reduce.3 = bf16[7168,64]{1,0:T(8,128)(2,1)} reduce(bf16[7168,1,64]{2,1,0:T(2,128)(2,1)} %bitcast.94, bf16[]{:T(256)} %broadcast.46), dimensions={1}, to_apply=%bitcast.72.reduce_sub_computation | reduce | bytes 1835010
  159.7 4.3 reshape.70
  163.9 7.2 %all-to-all-start.1 = ((bf16[16,2,14336]{2,1,0:T(2,128)(2,1)}), bf16[16,2,14336]{2,1,0:T(2,128)(2,1)}, u32[]{:S(2)}, u32[]{:S(2)}) async-start(bf16[16,2,14336]{2,1,0:T(2,128)(2,1)} %reshape.70), calls=%async_computation.1 | async-start | bytes 1835008 | tf_op jit(solution)/shard_map/all_to_all | solution.py:45
  171.6 9.9 %reshape.69 = bf16[7168,1,64]{2,1,0:T(2,128)(2,1)} reshape(bf16[16,2,14336]{2,1,0:T(2,128)(2,1)} %all-to-all-done.3) | data formatting | bytes 1835008
  181.5 8.1 %copy.88 = bf16[1,64,7168]{2,1,0:T(8,128)(2,1)} copy(bf16[1,64,7168]{1,0,2:T(2,128)(2,1)} %bitcast.95) | data formatting | bytes 1835008 | tf_op jit(solution)/shard_map/all_to_all | solution.py:52
  189.7 2.3 all_to_all.84
  192.0 1.6 copy.89
  193.6 9.9 %reshape.71 = bf16[7168,1,64]{2,1,0:T(2,128)(2,1)} reshape(bf16[16,2,14336]{2,1,0:T(2,128)(2,1)} %all-to-all-done.1) | data formatting | bytes 1835008
  203.5 8.1 %copy.84 = bf16[1,64,7168]{2,1,0:T(8,128)(2,1)} copy(bf16[1,64,7168]{1,0,2:T(2,128)(2,1)} %bitcast.96) | data formatting | bytes 1835008 | tf_op jit(solution)/shard_map/all_to_all | solution.py:45
  211.7 2.3 all_to_all.77
  214.6 2.3 convolution_convert_fusion.1
  217.0 2.3 convolution_convert_fusion.2
  219.4 2.3 convolution_convert_fusion
  221.7 11.3 %pad_maximum_fusion = bf16[1024,6144]{1,0:T(8,128)(2,1)} fusion(bf16[1024,2048]{1,0:T(8,128)(2,1)S(1)} %convolution_convert_fusion, bf16[1024,2048]{1,0:T(8,128)(2,1)S(1)} %convolution_convert_fusion.1, bf16[1024,2048]{1,0:T(8,128)(2,1)S(1)} %convolution_convert_fusion.2), kind=kLoop, calls=%fused_computation | loop fusion | flops 37748736 | bytes 25165824 | tf_op jit(solution)/shard_map/concatenate | solution.py:72
  234.0 122.2 %reduce-scatter.2.cloned.1.call-done = bf16[64,6144]{1,0:T(8,128)(2,1)} async-done(((bf16[1024,6144]{1,0:T(8,128)(2,1)}), bf16[64,6144]{1,0:T(8,128)(2,1)}) %reduce-scatter.2.cloned.1.call-update) | async-done | bytes 786448 | tf_op jit(solution)/shard_map/reduce_scatter | solution.py:71
  358.8 91.2 %all-gather.2.cloned.1.call-done = bf16[1024,6144]{1,0:T(8,128)(2,1)} async-done(((bf16[64,6144]{1,0:T(8,128)(2,1)}), bf16[1024,6144]{1,0:T(8,128)(2,1)}) %all-gather.2.cloned.1.call-update) | async-done | bytes 12582928 | tf_op jit(solution)/shard_map/all_gather | solution.py:85
  449.9 4.4 fusion.4
  454.3 4.4 fusion.34
  458.7 3.9 copy.90
  462.6 8.3 %reduce.4 = bf16[1024,448]{1,0:T(8,128)(2,1)S(1)} reduce(bf16[1024,1,448]{2,1,0:T(2,128)(2,1)} %bitcast.98, bf16[]{:T(256)} %broadcast.46), dimensions={1}, to_apply=%bitcast.74.reduce_sub_computation | reduce | bytes 1835010
  470.9 2.1 reshape.72
  473.0 3.9 all-to-all-start.4
  476.9 5.8 fusion.16
  482.7 10.2 %all-to-all-done.4 = bf16[16,2,14336]{2,1,0:T(2,128)(2,1)S(1)} async-done(((bf16[16,2,14336]{2,1,0:T(2,128)(2,1)}), bf16[16,2,14336]{2,1,0:T(2,128)(2,1)S(1)}, u32[]{:S(2)}, u32[]{:S(2)}) %all-to-all-start.4) | async-done | bytes 917536 | tf_op jit(solution)/shard_map/all_to_all | solution.py:100
  492.9 3.7 reshape.73
  496.6 1.9 copy.102
  498.5 1.7 copy.98
  500.2 11.1 %reshape.66 = bf16[1,64,7168]{1,0,2:T(2,128)(2,1)} reshape(bf16[1,64,16,448]{1,3,2,0:T(8,128)(2,1)} %copy.98) | data formatting | bytes 1835008 | tf_op jit(solution)/shard_map/all_to_all | solution.py:100
  511.3 41.0 %reduce.5 = bf16[7168,64]{1,0:T(8,128)(2,1)} reduce(bf16[7168,1,64]{2,1,0:T(2,128)(2,1)} %bitcast.93, bf16[]{:T(256)} %broadcast.46), dimensions={1}, to_apply=%bitcast.76.reduce_sub_computation | reduce | bytes 1835010
  552.3 4.3 reshape.74
  556.6 4.4 all-to-all-start.5
  561.0 5.9 fusion.19
  566.9 5.5 fusion.22
  572.5 2.9 all-to-all-done.5
  575.4 4.1 reshape.75
  579.5 7.2 %copy.93 = bf16[1,64,7168]{2,1,0:T(8,128)(2,1)S(1)} copy(bf16[1,64,7168]{1,0,2:T(2,128)(2,1)} %bitcast.97) | data formatting | bytes 1835008 | tf_op jit(solution)/shard_map/all_to_all | solution.py:99
  (51 shorter events, 10.5 us)
Async XLA Ops:
  7.2 207.4 %copy-start = (bf16[1,448,2048]{2,1,0:T(8,128)(2,1)S(1)}, bf16[1,448,2048]{2,1,0:T(8,128)(2,1)}, u32[]{:S(2)}) copy-start(bf16[1,448,2048]{2,1,0:T(8,128)(2,1)} %param.12) | copy-start | bytes 5505028
  7.2 11.8 %copy-start.5 = (bf16[128,896]{1,0:T(8,128)(2,1)S(1)}, bf16[128,896]{1,0:T(8,128)(2,1)}, u32[]{:S(2)}) copy-start(bf16[128,896]{1,0:T(8,128)(2,1)} %param.7) | copy-start | bytes 688132
  12.6 20.8 %all-to-all-start.2 = ((bf16[8,64,896]{2,1,0:T(8,128)(2,1)}), bf16[8,64,896]{2,1,0:T(8,128)(2,1)S(1)}, u32[]{:S(2)}, u32[]{:S(2)}) async-start(bf16[8,64,896]{2,1,0:T(8,128)(2,1)} %bitcast.12), calls=%async_computation.2 | async-start | bytes 1835008 | tf_op jit(solution)/shard_map/all_to_all | solution.py:53
  33.4 0.9 copy-start.1
  34.3 63.0 %all-to-all-start = ((bf16[8,64,896]{2,1,0:T(8,128)(2,1)}), bf16[8,64,896]{2,1,0:T(8,128)(2,1)S(1)}, u32[]{:S(2)}, u32[]{:S(2)}) async-start(bf16[8,64,896]{2,1,0:T(8,128)(2,1)} %bitcast.5), calls=%async_computation | async-start | bytes 1835008 | tf_op jit(solution)/shard_map/all_to_all | solution.py:46
  97.3 66.6 %all-to-all-start.3 = ((bf16[16,2,14336]{2,1,0:T(2,128)(2,1)}), bf16[16,2,14336]{2,1,0:T(2,128)(2,1)}, u32[]{:S(2)}, u32[]{:S(2)}) async-start(bf16[16,2,14336]{2,1,0:T(2,128)(2,1)} %reshape.68), calls=%async_computation.3 | async-start | bytes 1835008 | tf_op jit(solution)/shard_map/all_to_all | solution.py:52
  163.9 29.7 %all-to-all-start.1 = ((bf16[16,2,14336]{2,1,0:T(2,128)(2,1)}), bf16[16,2,14336]{2,1,0:T(2,128)(2,1)}, u32[]{:S(2)}, u32[]{:S(2)}) async-start(bf16[16,2,14336]{2,1,0:T(2,128)(2,1)} %reshape.70), calls=%async_computation.1 | async-start | bytes 1835008 | tf_op jit(solution)/shard_map/all_to_all | solution.py:45
  171.2 185.0 %reduce-scatter.2.cloned.1.call-start = ((), (), s32[]{:S(2)}) async-start(), calls=%async_computation.7 | async-start | bytes 13369344 | tf_op jit(solution)/shard_map/reduce_scatter | solution.py:71
  214.6 2.4 copy-start.4
  214.6 2.4 copy-start.7
  217.0 2.4 copy-start.2
  217.0 2.4 copy-start.6
  233.0 0.7 copy-start.9
  233.0 216.9 %all-gather.2.cloned.1.call-start = ((), (), s32[]{:S(2)}) async-start(), calls=%async_computation.8 | async-start | bytes 13369344 | tf_op jit(solution)/shard_map/all_gather | solution.py:85
  449.9 4.4 copy-start.8
  473.0 19.9 %all-to-all-start.4 = ((bf16[16,2,14336]{2,1,0:T(2,128)(2,1)}), bf16[16,2,14336]{2,1,0:T(2,128)(2,1)S(1)}, u32[]{:S(2)}, u32[]{:S(2)}) async-start(bf16[16,2,14336]{2,1,0:T(2,128)(2,1)} %reshape.72), calls=%async_computation.5 | async-start | bytes 1835008 | tf_op jit(solution)/shard_map/all_to_all | solution.py:100
  556.6 18.8 %all-to-all-start.5 = ((bf16[8,2,28672]{2,1,0:T(2,128)(2,1)}), bf16[8,2,28672]{2,1,0:T(2,128)(2,1)S(1)}, u32[]{:S(2)}, u32[]{:S(2)}) async-start(bf16[8,2,28672]{2,1,0:T(2,128)(2,1)} %reshape.74), calls=%async_computation.6 | async-start | bytes 1835008 | tf_op jit(solution)/shard_map/all_to_all | solution.py:99
  561.0 5.9 copy-start.3
Sparse Core Ops, SparseCore 0:
  233.1 123.0 reduce-scatter.1
  359.5 90.3 all-gather.1
where the time goes:
time: 606 us; the launch traced here: 595 us
  waiting for transfers between devices  240 us (40%)
  other arithmetic  147 us (24%)
  local copies, waits for them, and re-layouts  122 us (20%)
  matrix products  37.9 us (6%)
  starting transfers between devices  34.6 us (6%)
  between operations  14.8 us (2%)
    unnamed x4, other arithmetic  131 us
    reduce_scatter x1, waiting for transfers between devices, body(): lax.psum_scatter(jnp.concatenate([gate, upper, back], axis=1).astype(jnp....  122 us
    all_gather x1, waiting for transfers between devices, body(): piece = lax.all_gather(local, 'dp', axis=0, tiled=True)  91.2 us
    unnamed x32, local copies, waits for them, and re-layouts  47.4 us
    all_to_all x2, local copies, waits for them, and re-layouts, body(): lax.all_to_all(send_g, 'expert', split_axis=0, concat_axis=2, tiled=True)  13.7 us
    all_to_all x1, waiting for transfers between devices, body(): lax.all_to_all(send_g, 'expert', split_axis=0, concat_axis=2, tiled=True)  13.1 us
    all_to_all x2, local copies, waits for them, and re-layouts, body(): lax.all_to_all(dx_rows.reshape(1, slots, shard_width), 'dp', split_axis=1...  12.8 us
    all_to_all x2, local copies, waits for them, and re-layouts, body(): lax.all_to_all(send_x, 'expert', split_axis=0, concat_axis=2, tiled=True)  12.8 us
  transfers between devices with their start and end apart: 8, of which 5 were waited for; matrix products, arithmetic and copies ran while one was open for 26% of the time, Pallas kernels for 0%

commit v1 on v0

--- a/solution.py
+++ b/solution.py
@@ -96,14 +96,26 @@
     ) + lax.dot_general(d_up, up_shard, last_dims, preferred_element_type=jnp.float32)
     dx_rows = block_dx.astype(jnp.bfloat16)
     grad_g, grad_u, grad_d, dx_rows = (grad_g, grad_u, grad_d, dx_rows)
-    returned = lax.all_to_all(
+    returned = jnp.concatenate(
         lax.all_to_all(
-            dx_rows.reshape(1, slots, shard_width), "dp", split_axis=1, concat_axis=2, tiled=True
+            jnp.stack(
+                jnp.split(
+                    lax.all_to_all(
+                        dx_rows.reshape(1, slots, shard_width),
+                        "dp",
+                        split_axis=1,
+                        concat_axis=2,
+                        tiled=True,
+                    ),
+                    lax.axis_size("expert"),
+                    axis=2,
+                )
+            ),
+            "expert",
+            0,
+            0,
         ),
-        "expert",
-        split_axis=2,
-        concat_axis=0,
-        tiled=True,
+        axis=0,
     )
     returned = returned.reshape(experts * capacity, -1)
     grad_tokens = lax.dot_general(

time: 606 us -> 551 us (0.909)
  other arithmetic: 147 us -> 106 us
  local copies, waits for them, and re-layouts: 122 us -> 108 us
    unnamed x4 -> x3, other arithmetic: 131 us -> 90.3 us
    all_to_all x2, local copies, waits for them, and re-layouts: 12.8 us -> 2.69 us  [body(): lax.all_to_all(dx_rows.reshape(1, slots, shard_width), 'dp', split_axis=1...]
    all_to_all x3 -> x0, local copies, waits for them, and re-layouts: 7.39 us -> none  [body(): lax.all_to_all(lax.all_to_all(dx_rows.reshape(1, slots, shard_width), 'dp...]
    unnamed x32 -> x36, local copies, waits for them, and re-layouts: 47.4 us -> 49.5 us
  transfers between devices with their start and end apart: 8 -> 8, of which waited for: 5 -> 5; matrix products, arithmetic and copies ran while one was open for 26% -> 29% of each run, Pallas kernels for 0% -> 0%
where the time goes in v1:
time: 551 us; the launch traced here: 540 us
  waiting for transfers between devices  240 us (44%)
  local copies, waits for them, and re-layouts  108 us (20%)
  other arithmetic  106 us (19%)
  matrix products  37.9 us (7%)
  starting transfers between devices  34.3 us (6%)
  between operations  14.5 us (3%)
    reduce_scatter x1, waiting for transfers between devices, body(): lax.psum_scatter(jnp.concatenate([gate, upper, back], axis=1).astype(jnp....  122 us
    all_gather x1, waiting for transfers between devices, body(): piece = lax.all_gather(local, 'dp', axis=0, tiled=True)  91.1 us
    unnamed x3, other arithmetic  90.3 us
    unnamed x36, local copies, waits for them, and re-layouts  49.5 us
    all_to_all x2, local copies, waits for them, and re-layouts, body(): lax.all_to_all(send_g, 'expert', split_axis=0, concat_axis=2, tiled=True)  13.7 us
    all_to_all x1, waiting for transfers between devices, body(): lax.all_to_all(send_g, 'expert', split_axis=0, concat_axis=2, tiled=True)  13.1 us
    all_to_all x2, local copies, waits for them, and re-layouts, body(): lax.all_to_all(send_x, 'expert', split_axis=0, concat_axis=2, tiled=True)  12.8 us
    all_to_all x3, local copies, waits for them, and re-layouts, body(): lax.all_to_all(lax.all_to_all(send_g, 'expert', split_axis=0, concat_axis...  12 us
  transfers between devices with their start and end apart: 8, of which 5 were waited for; matrix products, arithmetic and copies ran while one was open for 29% of the time, Pallas kernels for 0%

profile of v1, /device:TPU:1, one launch (start us, length us, event | category | flops | bytes accessed | tf_op | source)
XLA Modules:
  0.0 540.1 jit_solution(3937796443249993849)
XLA Ops:
  10.3 2.2 convolution_convert_fusion.3
  12.6 6.4 %all-to-all-start.2 = ((bf16[8,64,896]{2,1,0:T(8,128)(2,1)}), bf16[8,64,896]{2,1,0:T(8,128)(2,1)S(1)}, u32[]{:S(2)}, u32[]{:S(2)}) async-start(bf16[8,64,896]{2,1,0:T(8,128)(2,1)} %bitcast.12), calls=%async_computation.2 | async-start | bytes 1835008 | tf_op jit(solution)/shard_map/all_to_all | solution.py:53
  20.3 13.1 %all-to-all-done.2 = bf16[8,64,896]{2,1,0:T(8,128)(2,1)S(1)} async-done(((bf16[8,64,896]{2,1,0:T(8,128)(2,1)}), bf16[8,64,896]{2,1,0:T(8,128)(2,1)S(1)}, u32[]{:S(2)}, u32[]{:S(2)}) %all-to-all-start.2) | async-done | bytes 917536 | tf_op jit(solution)/shard_map/all_to_all | solution.py:53
  34.3 3.6 all-to-all-start
  37.9 2.6 copy.86
  40.4 11.1 %reshape.60 = bf16[1,64,7168]{1,0,2:T(2,128)(2,1)} reshape(bf16[1,64,8,896]{1,3,2,0:T(8,128)(2,1)} %copy.86) | data formatting | bytes 1835008 | tf_op jit(solution)/shard_map/all_to_all | solution.py:53
  52.1 41.0 %reduce.2 = bf16[7168,64]{1,0:T(8,128)(2,1)} reduce(bf16[7168,1,64]{2,1,0:T(2,128)(2,1)} %bitcast.112, bf16[]{:T(256)} %broadcast.46), dimensions={1}, to_apply=%bitcast.93.reduce_sub_computation | reduce | bytes 1835010
  93.1 4.3 reshape.62
  97.4 8.5 %all-to-all-start.3 = ((bf16[16,2,14336]{2,1,0:T(2,128)(2,1)}), bf16[16,2,14336]{2,1,0:T(2,128)(2,1)}, u32[]{:S(2)}, u32[]{:S(2)}) async-start(bf16[16,2,14336]{2,1,0:T(2,128)(2,1)} %reshape.62), calls=%async_computation.3 | async-start | bytes 1835008 | tf_op jit(solution)/shard_map/all_to_all | solution.py:52
  105.9 1.7 copy.85
  107.5 11.1 %reshape.59 = bf16[1,64,7168]{1,0,2:T(2,128)(2,1)} reshape(bf16[1,64,8,896]{1,3,2,0:T(8,128)(2,1)} %copy.85) | data formatting | bytes 1835008 | tf_op jit(solution)/shard_map/all_to_all | solution.py:46
  118.6 41.0 %reduce.3 = bf16[7168,64]{1,0:T(8,128)(2,1)} reduce(bf16[7168,1,64]{2,1,0:T(2,128)(2,1)} %bitcast.113, bf16[]{:T(256)} %broadcast.46), dimensions={1}, to_apply=%bitcast.95.reduce_sub_computation | reduce | bytes 1835010
  159.6 4.3 reshape.64
  163.9 7.2 %all-to-all-start.1 = ((bf16[16,2,14336]{2,1,0:T(2,128)(2,1)}), bf16[16,2,14336]{2,1,0:T(2,128)(2,1)}, u32[]{:S(2)}, u32[]{:S(2)}) async-start(bf16[16,2,14336]{2,1,0:T(2,128)(2,1)} %reshape.64), calls=%async_computation.1 | async-start | bytes 1835008 | tf_op jit(solution)/shard_map/all_to_all | solution.py:45
  171.4 9.9 %reshape.63 = bf16[7168,1,64]{2,1,0:T(2,128)(2,1)} reshape(bf16[16,2,14336]{2,1,0:T(2,128)(2,1)} %all-to-all-done.3) | data formatting | bytes 1835008
  181.3 8.1 %copy.80 = bf16[1,64,7168]{2,1,0:T(8,128)(2,1)} copy(bf16[1,64,7168]{1,0,2:T(2,128)(2,1)} %bitcast.114) | data formatting | bytes 1835008 | tf_op jit(solution)/shard_map/all_to_all | solution.py:52
  189.5 2.3 all_to_all.76
  191.8 1.5 copy.81
  193.4 9.9 %reshape.65 = bf16[7168,1,64]{2,1,0:T(2,128)(2,1)} reshape(bf16[16,2,14336]{2,1,0:T(2,128)(2,1)} %all-to-all-done.1) | data formatting | bytes 1835008
  203.3 8.1 %copy.76 = bf16[1,64,7168]{2,1,0:T(8,128)(2,1)} copy(bf16[1,64,7168]{1,0,2:T(2,128)(2,1)} %bitcast.115) | data formatting | bytes 1835008 | tf_op jit(solution)/shard_map/all_to_all | solution.py:45
  211.4 2.3 all_to_all.69
  214.4 2.3 convolution_convert_fusion.1
  216.8 2.3 convolution_convert_fusion.2
  219.1 2.3 convolution_convert_fusion
  221.5 11.5 %pad_maximum_fusion = bf16[1024,6144]{1,0:T(8,128)(2,1)} fusion(bf16[1024,2048]{1,0:T(8,128)(2,1)S(1)} %convolution_convert_fusion, bf16[1024,2048]{1,0:T(8,128)(2,1)S(1)} %convolution_convert_fusion.1, bf16[1024,2048]{1,0:T(8,128)(2,1)S(1)} %convolution_convert_fusion.2), kind=kLoop, calls=%fused_computation | loop fusion | flops 37748736 | bytes 25165824 | tf_op jit(solution)/shard_map/concatenate | solution.py:72
  233.9 122.2 %reduce-scatter.2.cloned.1.call-done = bf16[64,6144]{1,0:T(8,128)(2,1)} async-done(((bf16[1024,6144]{1,0:T(8,128)(2,1)}), bf16[64,6144]{1,0:T(8,128)(2,1)}) %reduce-scatter.2.cloned.1.call-update) | async-done | bytes 786448 | tf_op jit(solution)/shard_map/reduce_scatter | solution.py:71
  358.7 91.1 %all-gather.2.cloned.1.call-done = bf16[1024,6144]{1,0:T(8,128)(2,1)} async-done(((bf16[64,6144]{1,0:T(8,128)(2,1)}), bf16[1024,6144]{1,0:T(8,128)(2,1)}) %all-gather.2.cloned.1.call-update) | async-done | bytes 12582928 | tf_op jit(solution)/shard_map/all_gather | solution.py:85
  449.9 4.4 fusion.4
  454.3 4.4 fusion.34
  458.7 3.9 copy.82
  462.6 8.3 %reduce.4 = bf16[1024,448]{1,0:T(8,128)(2,1)S(1)} reduce(bf16[1024,1,448]{2,1,0:T(2,128)(2,1)} %bitcast.116, bf16[]{:T(256)} %broadcast.46), dimensions={1}, to_apply=%bitcast.97.reduce_sub_computation | reduce | bytes 1835010
  470.8 2.1 reshape.66
  472.9 3.8 all-to-all-start.4
  476.8 5.8 %fusion.16 = bf16[1,448,2048]{2,1,0:T(8,128)(2,1)} fusion(bf16[1024,448]{1,0:T(8,128)(2,1)} %bitcast.128, bf16[1024,6144]{1,0:T(8,128)(2,1)} %all-gather.2.cloned.1.call-done), kind=kOutput, calls=%fused_computation.17 | convolution fusion | flops 1880883200 | bytes 7077888 | tf_op jit(solution)/shard_map/dot_general | solution.py:91
  482.6 10.2 %all-to-all-done.4 = bf16[16,2,14336]{2,1,0:T(2,128)(2,1)S(1)} async-done(((bf16[16,2,14336]{2,1,0:T(2,128)(2,1)}), bf16[16,2,14336]{2,1,0:T(2,128)(2,1)S(1)}, u32[]{:S(2)}, u32[]{:S(2)}) %all-to-all-start.4) | async-done | bytes 917536 | tf_op jit(solution)/shard_map/all_to_all | solution.py:103
  492.8 3.7 reshape.67
  496.5 1.9 copy.89
  499.0 2.1 all_to_all.81
  501.1 1.6 fusion.48
  502.7 1.6 fusion.47
  505.8 1.5 fusion.45
  507.3 1.6 fusion.44
  510.4 1.6 fusion.42
  512.0 1.6 fusion.41
  513.5 4.1 all-to-all-start.5
  517.6 5.9 %fusion.19 = bf16[1,448,2048]{2,1,0:T(8,128)(2,1)} fusion(bf16[1024,448]{1,0:T(8,128)(2,1)} %bitcast.129, bf16[1024,6144]{1,0:T(8,128)(2,1)} %all-gather.2.cloned.1.call-done), kind=kOutput, calls=%fused_computation.18 | convolution fusion | flops 1880883200 | bytes 7077888 | tf_op jit(solution)/shard_map/dot_general | solution.py:92
  523.6 5.5 %fusion.22 = bf16[1,2048,448]{1,2,0:T(8,128)(2,1)} fusion(bf16[1024,448]{1,0:T(8,128)(2,1)S(1)} %bitcast.125, bf16[1024,6144]{1,0:T(8,128)(2,1)} %all-gather.2.cloned.1.call-done), kind=kOutput, calls=%fused_computation.19 | convolution fusion | flops 1880883200 | bytes 6946816 | tf_op jit(solution)/shard_map/dot_general | solution.py:93
  529.1 2.9 all-to-all-done.5
  (52 shorter events, 14.9 us)
Async XLA Ops:
  7.2 207.2 %copy-start = (bf16[1,448,2048]{2,1,0:T(8,128)(2,1)S(1)}, bf16[1,448,2048]{2,1,0:T(8,128)(2,1)}, u32[]{:S(2)}) copy-start(bf16[1,448,2048]{2,1,0:T(8,128)(2,1)} %param.12) | copy-start | bytes 5505028
  7.2 11.8 %copy-start.5 = (bf16[128,896]{1,0:T(8,128)(2,1)S(1)}, bf16[128,896]{1,0:T(8,128)(2,1)}, u32[]{:S(2)}) copy-start(bf16[128,896]{1,0:T(8,128)(2,1)} %param.7) | copy-start | bytes 688132
  12.6 20.8 %all-to-all-start.2 = ((bf16[8,64,896]{2,1,0:T(8,128)(2,1)}), bf16[8,64,896]{2,1,0:T(8,128)(2,1)S(1)}, u32[]{:S(2)}, u32[]{:S(2)}) async-start(bf16[8,64,896]{2,1,0:T(8,128)(2,1)} %bitcast.12), calls=%async_computation.2 | async-start | bytes 1835008 | tf_op jit(solution)/shard_map/all_to_all | solution.py:53
  33.4 0.9 copy-start.1
  34.3 63.1 %all-to-all-start = ((bf16[8,64,896]{2,1,0:T(8,128)(2,1)}), bf16[8,64,896]{2,1,0:T(8,128)(2,1)S(1)}, u32[]{:S(2)}, u32[]{:S(2)}) async-start(bf16[8,64,896]{2,1,0:T(8,128)(2,1)} %bitcast.5), calls=%async_computation | async-start | bytes 1835008 | tf_op jit(solution)/shard_map/all_to_all | solution.py:46
  97.4 66.6 %all-to-all-start.3 = ((bf16[16,2,14336]{2,1,0:T(2,128)(2,1)}), bf16[16,2,14336]{2,1,0:T(2,128)(2,1)}, u32[]{:S(2)}, u32[]{:S(2)}) async-start(bf16[16,2,14336]{2,1,0:T(2,128)(2,1)} %reshape.62), calls=%async_computation.3 | async-start | bytes 1835008 | tf_op jit(solution)/shard_map/all_to_all | solution.py:52
  163.9 29.4 %all-to-all-start.1 = ((bf16[16,2,14336]{2,1,0:T(2,128)(2,1)}), bf16[16,2,14336]{2,1,0:T(2,128)(2,1)}, u32[]{:S(2)}, u32[]{:S(2)}) async-start(bf16[16,2,14336]{2,1,0:T(2,128)(2,1)} %reshape.64), calls=%async_computation.1 | async-start | bytes 1835008 | tf_op jit(solution)/shard_map/all_to_all | solution.py:45
  171.1 185.0 %reduce-scatter.2.cloned.1.call-start = ((), (), s32[]{:S(2)}) async-start(), calls=%async_computation.7 | async-start | bytes 13369344 | tf_op jit(solution)/shard_map/reduce_scatter | solution.py:71
  214.4 2.4 copy-start.4
  214.4 2.4 copy-start.7
  216.8 2.4 copy-start.2
  216.8 2.4 copy-start.6
  233.0 0.7 copy-start.9
  233.0 216.9 %all-gather.2.cloned.1.call-start = ((), (), s32[]{:S(2)}) async-start(), calls=%async_computation.8 | async-start | bytes 13369344 | tf_op jit(solution)/shard_map/all_gather | solution.py:85
  449.9 4.4 copy-start.8
  472.9 19.9 %all-to-all-start.4 = ((bf16[16,2,14336]{2,1,0:T(2,128)(2,1)}), bf16[16,2,14336]{2,1,0:T(2,128)(2,1)S(1)}, u32[]{:S(2)}, u32[]{:S(2)}) async-start(bf16[16,2,14336]{2,1,0:T(2,128)(2,1)} %reshape.66), calls=%async_computation.5 | async-start | bytes 1835008 | tf_op jit(solution)/shard_map/all_to_all | solution.py:103
  513.5 18.5 %all-to-all-start.5 = ((bf16[8,1,64,896]{3,2,1,0:T(8,128)(2,1)}), bf16[8,1,64,896]{3,2,1,0:T(8,128)(2,1)S(1)}, u32[]{:S(2)}, u32[]{:S(2)}) async-start(bf16[8,1,64,896]{3,2,1,0:T(8,128)(2,1)} %fusion.41), calls=%async_computation.6 | async-start | bytes 1835008 | tf_op jit(solution)/shard_map/all_to_all | solution.py:100
  517.6 5.9 %copy-start.3 = (bf16[1,16,64,448]{3,2,1,0:T(8,128)(2,1)S(1)}, bf16[1,16,64,448]{3,2,1,0:T(8,128)(2,1)}, u32[]{:S(2)}) copy-start(bf16[1,16,64,448]{3,2,1,0:T(8,128)(2,1)} %copy.81) | copy-start | bytes 2752516
Sparse Core Ops, SparseCore 0:
  233.1 123.0 reduce-scatter.1
  359.5 90.3 all-gather.1
